TPU v7x, 32 devices: a whole 2x2x4 slice. The times are simulated.
32 devices in a mesh: prow: 8 (over z, x), pcol: 4 (over y, core).
Axes of the slice: x: 2, y: 2, z: 4, core: 2. Of those that a mesh axis runs over, the one named last changes fastest.
Arguments:
- slab: float32 [4096, 2048], P('prow', 'pcol'), may hold values from -6 to 6
- panel: float32 [4096, 512], P('prow', 'pcol'), may hold values from -0.25 to 0.25
- tri_inverse: float32 [512, 512], replicated, as said below
- pivots: int32 [512], replicated, may hold values from 512 to 4095, as said below
Outputs:
- updated: float32 [4096, 2048], P('prow', 'pcol')
Inputs may be any that keep to these rules, and one draw needn't show every extreme that they name: The pivots are distinct row numbers of the rows below the first 512. At most 75 of them fall among the 512 rows of one device, and some device holds exactly 75. `tri_inverse`: lower triangular with zeros above the diagonal; the diagonal lies between 0.8 and 1.2.
All inputs are finite; a program needn't handle non-finite values.
Results may differ from a plain program's by a relative error of at most 0.000053.
Values sent between devices are 32-bit elements; how exact they have to be, the bound alone decides.
No kernel may reach another device: no remote copies, remote signals or barrier semaphores. Data moves between devices by JAX's collectives and lax.ppermute only.
A program may use at most 64 MiB of HBM per device.

v0:
```python
import functools

import jax
import jax.numpy as jnp
from jax import lax
from jax.experimental import pallas as pl
from jax.experimental.pallas import tpu as pltpu
from jax.sharding import PartitionSpec as P

F32 = jnp.float32
BF16 = jnp.bfloat16
VMEM_BYTES = 24 * 1024 * 1024
STORE_PARTS = 4
LANES = 128
SUBLANES = 8
PICK_US = 2
AFTER_US = 0.1
FACTOR_US = 1
RELAY_US = 20
ASSEMBLE_US = 20


def _cost(us):
    return pl.CostEstimate(flops=int(us * 1_000_000_000), bytes_accessed=0, transcendentals=0)


def _two_parts(x):
    high = x.astype(BF16)
    low = (x - high.astype(F32)).astype(BF16)
    return high, low


def _dot(a, b):
    return jnp.dot(a, b, preferred_element_type=F32)


def _dot_nt(a, b):
    return lax.dot_general(a, b, (((1,), (1,)), ((), ())), preferred_element_type=F32)


def _iota(shape, dim):
    return lax.broadcasted_iota(jnp.int32, shape, dim)


def _owners_and_ranks(piv, rows_dev, devices):
    count = piv.shape[1]
    owner = piv // rows_dev
    local = piv - owner * rows_dev
    is_owner = _iota((devices, count), 0) == owner
    earlier = (_iota((count, count), 0) < _iota((count, count), 1)).astype(BF16)
    ranks = _dot(is_owner.astype(BF16), earlier)
    rank = jnp.sum(jnp.where(is_owner, ranks, 0.0), axis=0, keepdims=True)
    return owner, local, rank.astype(jnp.int32)


def _select_rows(one_hot, parts):
    high, low = parts
    return _dot(one_hot, high) + _dot(one_hot, low)


class _Packing:
    def __init__(self, capacity, cols):
        self.tiles = cols // LANES
        self.main = capacity // SUBLANES * SUBLANES
        self.extra = capacity - self.main
        while self.extra * self.tiles % SUBLANES:
            self.extra += 1
        self.shape = ((self.main + self.extra) * self.tiles, LANES)

    def __repr__(self):
        return "packing"

    def parts(self):
        for tile in range(self.tiles):
            yield tile, tile * self.main, self.tiles * self.main + tile * self.extra

    def store(self, ref, rows):
        for tile, main_at, extra_at in self.parts():
            cols = slice(tile * LANES, (tile + 1) * LANES)
            if self.main:
                ref[pl.ds(main_at, self.main), :] = rows[: self.main, cols]
            if self.extra:
                ref[pl.ds(extra_at, self.extra), :] = rows[self.main : self.main + self.extra, cols]

    def load(self, ref, block):
        tiles = []
        for _, main_at, extra_at in self.parts():
            pieces = []
            if self.main:
                pieces.append(ref[pl.ds(main_at, self.main), :])
            if self.extra:
                pieces.append(ref[pl.ds(extra_at, self.extra), :])
            if block > self.main + self.extra:
                pieces.append(jnp.zeros((block - self.main - self.extra, LANES), F32))
            tiles.append(jnp.concatenate(pieces, axis=0))
        return jnp.concatenate(tiles, axis=1)


def _pick_kernel(devices, block, rows_dev, me_ref, piv_ref, pick_ref):
    me = me_ref[0]
    piv = piv_ref[...]
    count = piv.shape[1]
    owner, local, rank = _owners_and_ranks(piv, rows_dev, devices)

    @pl.when(me == 0)
    def _():
        slot = (owner - 1) * block + rank
        pick = (_iota(((devices - 1) * block, count), 0) == slot).astype(BF16)
        if count < rows_dev:
            pick = jnp.pad(pick, ((0, 0), (0, rows_dev - count)))
        pick_ref[...] = pick

    @pl.when(me != 0)
    def _():
        slot = jnp.where(owner == me, rank, -1)
        pick = (_iota((block, count), 0) == slot).astype(BF16)
        at_row = (_iota((rows_dev, count), 0) == local).astype(BF16)
        pick_ref[pl.ds(0, block), :] = _dot_nt(pick, at_row).astype(BF16)


def _outgoing_kernel(devices, block, packing, me_ref, pick_ref, slab_ref, *out_refs):
    me = me_ref[0]
    parts = _two_parts(slab_ref[...])

    @pl.when(me == 0)
    def _():
        rows = _select_rows(pick_ref[...], parts)
        for step in range(1, devices):
            packing.store(out_refs[step], rows[(step - 1) * block : step * block])
        out_refs[0][...] = jnp.zeros_like(out_refs[0])

    @pl.when(me != 0)
    def _():
        rows = _select_rows(pick_ref[pl.ds(0, block), :], parts)
        out_refs[0][...] = rows
        for step in range(1, devices):
            packing.store(out_refs[step], rows)


def _relay_kernel(senders, waits, me_ref, came_ref, *refs):
    refs = refs[waits:]
    out_ref = refs[-1]
    me = me_ref[0]
    usual = me >= 0
    for sender, ref in zip(senders, refs[:-1]):
        usual = usual & (me != sender)

        @pl.when(me == sender)
        def _():
            out_ref[...] = ref[...]

    @pl.when(usual)
    def _():
        out_ref[...] = came_ref[...]


def _after_kernel(panel_ref, _, out_ref):
    out_ref[...] = panel_ref[...]


def _factor_kernel(devices, block, order, early, crossed, pieces, me_ref, col_ref, piv_ref, slab_ref, tri_ref, *refs):
    panel_refs = refs[:pieces]
    high_early, low_early, high_late, low_late, kept_ref, panel_rel, tri_rel, w_ref = refs[pieces:]
    me = me_ref[0]
    rows_dev = slab_ref.shape[0]
    depth = panel_refs[0].shape[1]
    piv = piv_ref[...]
    count = piv.shape[1]
    owner, local, rank = _owners_and_ranks(piv, rows_dev, devices)

    @pl.when(me == 0)
    def _():
        w_ref[...] = tri_ref[...]

    @pl.when(me != 0)
    def _():
        for step in range(pieces):
            first = pl.multiple_of((col_ref[0] ^ step) * depth, depth)
            tri_rel[pl.ds(step * depth, depth), :] = tri_ref[pl.ds(first, depth), :]
            panel_rel[:, pl.ds(step * depth, depth)] = panel_refs[step][...]
        tri_high, tri_low = _two_parts(tri_rel[...])
        high, low = _two_parts(panel_rel[...])
        w_ref[...] = -((_dot(high, tri_low) + _dot(low, tri_high)) + _dot(high, tri_high))

    total = devices * block
    relative = owner ^ me
    lead_step = me
    for step in crossed:
        swapped = (me == 0) | (me == 1) | (me == step) | (me == step ^ 1)
        relative = jnp.where(swapped & ((relative ^ step) < 2), relative ^ 1, relative)
        lead_step = jnp.where(swapped & ((me ^ step) < 2), me ^ 1, lead_step)
    slot = rank
    lead_first = 0
    for place, step in enumerate(order):
        slot = jnp.where(relative == step, rank + place * block, slot)
        lead_first = jnp.where(lead_step == step, place * block, lead_first)
    place = (_iota((total, count), 0) == slot).astype(BF16)
    is_mine = owner == me
    lead_slot = jnp.where(is_mine, lead_first + rank, -1)
    lead = (_iota((total, count), 0) == lead_slot).astype(BF16)
    at_row = ((_iota((rows_dev, count), 0) == local) & is_mine).astype(F32)
    high, low = _two_parts(w_ref[...])
    at_row_bf16 = at_row.astype(BF16)
    split = early * block
    for rows, high_ref, low_ref in ((slice(0, split), high_early, low_early), (slice(split, total), high_late, low_late)):
        high_ref[...] = (_dot_nt(high, place[rows]) + _dot_nt(at_row_bf16, lead[rows])).astype(BF16)
        low_ref[...] = _dot_nt(low, place[rows]).astype(BF16)
    taken = jnp.sum(at_row, axis=1, keepdims=True)
    stays = (taken < 0.5) & (me != 0)
    kept_ref[...] = jnp.where(stays, slab_ref[...], 0.0)


def _split_rows(block, packing, block_refs, high_rows, low_rows):
    for place, ref in enumerate(block_refs):
        packed = ref.shape == packing.shape
        high, low = _two_parts(packing.load(ref, block) if packed else ref[...])
        high_rows[pl.ds(place * block, block), :] = high
        low_rows[pl.ds(place * block, block), :] = low


def _product(high, low, high_rows, low_rows):
    return (_dot(high, low_rows) + _dot(low, high_rows)) + _dot(high, high_rows)


def _assemble_kernel(block, packing, blocks, *refs):
    high_rows, low_rows = refs[blocks:]
    _split_rows(block, packing, refs[:blocks], high_rows, low_rows)


def _early_kernel(high_ref, low_ref, kept_ref, high_rows, low_rows, out_ref):
    out_ref[...] = kept_ref[...] + _product(high_ref[...], low_ref[...], high_rows[...], low_rows[...])


def _late_kernel(block, packing, blocks, high_ref, low_ref, base_ref, *refs):
    out_hbm, high_rows, low_rows, result, sems = refs[blocks:]
    _split_rows(block, packing, refs[:blocks], high_rows, low_rows)
    high, low = high_rows[...], low_rows[...]
    part = result.shape[0] // STORE_PARTS
    stores = []
    for i in range(STORE_PARTS):
        rows = pl.ds(i * part, part)
        result[rows, :] = base_ref[rows, :] + _product(high_ref[rows, :], low_ref[rows, :], high, low)
        stores.append(pltpu.make_async_copy(result.at[rows], out_hbm.at[rows], sems.at[i]))
        stores[-1].start()
    for store in stores:
        store.wait()


def per_device(slab, panel, tri_inverse, pivots):
    rows_dev, cols_dev = slab.shape
    count = pivots.shape[0]
    devices = lax.axis_size("prow")
    pieces = lax.axis_size("pcol")
    capacity = rows_dev // (devices - 1) + 2
    block = -(-capacity // 16) * 16
    me = lax.axis_index("prow").astype(jnp.int32).reshape(1)
    col = lax.axis_index("pcol").astype(jnp.int32).reshape(1)
    piv = pivots.reshape(1, count)
    params = pltpu.CompilerParams(vmem_limit_bytes=VMEM_BYTES)
    smem = pl.BlockSpec(memory_space=pltpu.SMEM)
    vmem = pl.BlockSpec(memory_space=pltpu.VMEM)
    hbm = pl.BlockSpec(memory_space=pltpu.HBM)

    relayed = list(range(4, devices, 2))
    crossed = [step for step in relayed if step % 4 == 2]
    packing = _Packing(capacity, cols_dev)
    packed_type = jax.ShapeDtypeStruct(packing.shape, F32)
    pick = pl.pallas_call(
        functools.partial(_pick_kernel, devices, block, rows_dev),
        out_shape=jax.ShapeDtypeStruct(((devices - 1) * block, rows_dev), BF16),
        in_specs=[smem, vmem],
        out_specs=vmem,
        compiler_params=params,
        cost_estimate=_cost(PICK_US),
        name="pick_rows",
    )(me, piv)
    outgoing = pl.pallas_call(
        functools.partial(_outgoing_kernel, devices, block, packing),
        out_shape=[jax.ShapeDtypeStruct((block, cols_dev), F32)] + [packed_type] * (devices - 1),
        in_specs=[smem, vmem, vmem],
        out_specs=[vmem] * devices,
        compiler_params=params,
        name="outgoing_rows",
    )(me, pick, slab)

    def swap(x, axis, size, step):
        return lax.ppermute(x, axis, [(i, i ^ step) for i in range(size)])

    direct = [1, 2] + relayed + [3]
    rows = {0: outgoing[0]}
    for step in direct:
        if step in crossed:
            ends = {0: step ^ 1, 1: step, step: 1, step ^ 1: 0}
            pairs = [(i, ends.get(i, i ^ step)) for i in range(devices)]
            rows[step] = lax.ppermute(outgoing[step ^ 1], "prow", pairs)
        else:
            rows[step] = swap(outgoing[step], "prow", devices, step)
    order = [0] + direct + [step ^ 1 for step in relayed]
    early = 1 + len(direct)
    late = devices - early
    panel = pl.pallas_call(
        _after_kernel,
        out_shape=jax.ShapeDtypeStruct(panel.shape, F32),
        in_specs=[vmem, pl.BlockSpec(memory_space=pl.ANY)],
        out_specs=vmem,
        compiler_params=params,
        cost_estimate=_cost(AFTER_US),
        name="panel_after",
    )(panel, rows[2])
    panels = {0: panel}
    for step in range(2, pieces, 2):
        panels[step] = swap(panels[0], "pcol", pieces, step)
    for step in range(0, pieces, 2):
        panels[step ^ 1] = swap(panels[step], "pcol", pieces, 1)

    high_early, low_early, high_late, low_late, kept = pl.pallas_call(
        functools.partial(_factor_kernel, devices, block, order, early, crossed, pieces),
        out_shape=[jax.ShapeDtypeStruct((rows_dev, k * block), BF16) for k in (early, early, late, late)]
        + [jax.ShapeDtypeStruct((rows_dev, cols_dev), F32)],
        in_specs=[smem, smem, vmem, vmem, vmem] + [vmem] * pieces,
        out_specs=[vmem] * 5,
        scratch_shapes=[
            pltpu.VMEM((rows_dev, count), F32),
            pltpu.VMEM((count, count), F32),
            pltpu.VMEM((rows_dev, count), F32),
        ],
        compiler_params=params,
        cost_estimate=_cost(FACTOR_US),
        name="left_factor",
    )(me, col, piv, slab, tri_inverse, *[panels[s] for s in range(pieces)])

    for step in relayed:
        other = step ^ 1
        if step in crossed:
            ends = {0: step, other: 1}
            blocks = {0: outgoing[step], other: outgoing[step]}
        else:
            ends = {0: other, step: 1}
            blocks = {0: outgoing[other], step: outgoing[other]}
        waits = [rows[1], rows[3]] if step == relayed[0] else []
        passed = pl.pallas_call(
            functools.partial(_relay_kernel, list(blocks), len(waits)),
            out_shape=packed_type,
            in_specs=[smem, vmem] + [pl.BlockSpec(memory_space=pl.ANY)] * len(waits) + [vmem] * len(blocks),
            out_specs=vmem,
            compiler_params=params,
            cost_estimate=_cost(RELAY_US),
            name="relay",
        )(me, rows[step], *waits, *blocks.values())
        pairs = [(i, ends.get(i, i ^ 1)) for i in range(devices)]
        rows[other] = lax.ppermute(passed, "prow", pairs)

    result_type = jax.ShapeDtypeStruct((rows_dev, cols_dev), F32)
    high_rows, low_rows = pl.pallas_call(
        functools.partial(_assemble_kernel, block, packing, early),
        out_shape=[jax.ShapeDtypeStruct((early * block, cols_dev), BF16)] * 2,
        in_specs=[vmem] * early,
        out_specs=[vmem] * 2,
        compiler_params=params,
        cost_estimate=_cost(ASSEMBLE_US),
        name="assemble_rows",
    )(*[rows[s] for s in order[:early]])
    partial = pl.pallas_call(
        _early_kernel,
        out_shape=result_type,
        in_specs=[vmem] * 5,
        out_specs=vmem,
        compiler_params=params,
        name="early_rows",
    )(high_early, low_early, kept, high_rows, low_rows)
    return pl.pallas_call(
        functools.partial(_late_kernel, block, packing, late),
        out_shape=result_type,
        in_specs=[vmem] * (3 + late),
        out_specs=hbm,
        scratch_shapes=[pltpu.VMEM((late * block, cols_dev), BF16)] * 2
        + [pltpu.VMEM((rows_dev, cols_dev), F32), pltpu.SemaphoreType.DMA((STORE_PARTS,))],
        compiler_params=params,
        name="late_rows",
    )(high_late, low_late, partial, *[rows[s] for s in order[early:]])


def solution(mesh):
    return jax.shard_map(
        per_device,
        mesh=mesh,
        in_specs=(P("prow", "pcol"), P("prow", "pcol"), P(), P()),
        out_specs=P("prow", "pcol"),
        check_vma=False,
    )
```

profile of v0, /device:TPU:0, one launch (start us, length us, event | category | flops | bytes accessed | tf_op | source)
XLA Modules:
  0.0 30.5 jit_solution(7060935896202446384)
XLA Ops:
  0.0 0.0 copy-start.3
  0.0 0.7 %copy-done.3 = s32[512]{0:T(512)S(1)} copy-done((s32[512]{0:T(512)S(1)}, s32[512]{0:T(512)}, u32[]{:S(2)}) %copy-start.3) | copy-done | bytes 2072
  0.7 0.0 copy-start
  0.7 0.3 %pick_rows.1.pick_ref = bf16[560,512]{1,0:T(8,128)(2,1)S(1)} custom-call(s32[1]{0:T(128)} %bitcast.me_ref, s32[1,512]{1,0:T(1,128)S(1)} %bitcast.3), custom_call_target="tpu_custom_call" | custom-call | flops 2000000000 | tf_op jit(solution)/shard_map/pick_rows/pallas_call | solution.py:268
  1.0 0.9 %copy-done = f32[512,512]{1,0:T(8,128)S(1)} copy-done((f32[512,512]{1,0:T(8,128)S(1)}, f32[512,512]{1,0:T(8,128)}, u32[]{:S(2)}) %copy-start) | copy-done | bytes 1048600
  1.9 0.0 copy-start.1
  1.9 1.0 %outgoing_rows.1 = (f32[80,512]{1,0:T(8,128)S(1)}, f32[304,128]{1,0:T(8,128)S(1)}, f32[304,128]{1,0:T(8,128)S(1)}, f32[304,128]{1,0:T(8,128)S(1)}, f32[304,128]{...) custom-call(s32[1]{0:T(128)} %bitcast.me_ref, ...), custom_call_target="tpu_custom_call" | custom-call | tf_op jit(solution)/shard_map/outgoing_rows/pallas_call | solution.py:277
  2.9 2.7 %collective-permute-start = (f32[304,128]{1,0:T(8,128)S(1)}, f32[304,128]{1,0:T(8,128)S(1)}, u32[]{:S(2)}, u32[]{:S(2)}) collective-permute-start(f32[304,128]{1,0:T(8,128)S(1)} %get-tuple-element.20), channel_id=1, source_target_pairs={{0,8},{4,12},{8,0},{12,4},{16,24},{20,28},{24,16},{28,20},{1,9},{5... | collective-permute-start | bytes 466952 | tf_op jit(solution)/shard_map/ppermute | solution.py:287
  5.6 3.4 %collective-permute-start.6 = (f32[304,128]{1,0:T(8,128)S(1)}, f32[304,128]{1,0:T(8,128)S(1)}, u32[]{:S(2)}, u32[]{:S(2)}) collective-permute-start(f32[304,128]{1,0:T(8,128)S(1)} %get-tuple-element.29), channel_id=1, source_target_pairs={{0,28},{4,24},{8,16},{12,20},{16,8},{20,12},{24,4},{28,0},{1,29},{... | collective-permute-start | bytes 466952 | tf_op jit(solution)/shard_map/ppermute | solution.py:295
  9.0 0.5 %collective-permute-start.4 = (f32[304,128]{1,0:T(8,128)S(1)}, f32[304,128]{1,0:T(8,128)S(1)}, u32[]{:S(2)}, u32[]{:S(2)}) collective-permute-start(f32[304,128]{1,0:T(8,128)S(1)} %get-tuple-element.27), channel_id=1, source_target_pairs={{0,4},{4,0},{8,12},{12,8},{16,20},{20,16},{24,28},{28,24},{1,5},{5... | collective-permute-start | bytes 466952 | tf_op jit(solution)/shard_map/ppermute | solution.py:287
  9.5 0.1 collective-permute-start.5
  9.7 2.7 %collective-permute-start.7 = (f32[304,128]{1,0:T(8,128)S(1)}, f32[304,128]{1,0:T(8,128)S(1)}, u32[]{:S(2)}, u32[]{:S(2)}) collective-permute-start(f32[304,128]{1,0:T(8,128)S(1)} %get-tuple-element.30), channel_id=1, source_target_pairs={{0,12},{4,8},{8,4},{12,0},{16,28},{20,24},{24,20},{28,16},{1,13},{... | collective-permute-start | bytes 466952 | tf_op jit(solution)/shard_map/ppermute | solution.py:287
  12.4 0.0 collective-permute-done._.refs_2_
  12.4 0.0 copy-done.1
  12.4 1.6 %collective-permute-start.2 = (f32[512,128]{1,0:T(8,128)S(1)}, f32[512,128]{1,0:T(8,128)S(1)}, u32[]{:S(2)}, u32[]{:S(2)}) collective-permute-start(f32[512,128]{1,0:T(8,128)S(1)} %panel_after.1.refs_0_), channel_id=1, source_target_pairs={{0,2},{1,3},{2,0},{3,1},{4,6},{5,7},{6,4},{7,5},{8,10},{9,11},{10,... | collective-permute-start | bytes 786440 | tf_op jit(solution)/shard_map/ppermute | solution.py:287
  14.0 3.4 %collective-permute-done.6.refs_4_.came_ref = f32[304,128]{1,0:T(8,128)S(1)} collective-permute-done((f32[304,128]{1,0:T(8,128)S(1)}, f32[304,128]{1,0:T(8,128)S(1)}, u32[]{:S(2)}, u32[]{:S(2)}) %collective-permute-start.6) | collective-permute-done | bytes 155680 | tf_op jit(solution)/shard_map/ppermute | solution.py:295
  17.4 0.0 collective-permute-start.1
  17.4 3.5 %collective-permute-done.4.refs_1_.refs_0_ = f32[304,128]{1,0:T(8,128)S(1)} collective-permute-done((f32[304,128]{1,0:T(8,128)S(1)}, f32[304,128]{1,0:T(8,128)S(1)}, u32[]{:S(2)}, u32[]{:S(2)}) %collective-permute-start.4) | collective-permute-done | bytes 155680 | tf_op jit(solution)/shard_map/ppermute | solution.py:287
  20.9 1.3 %collective-permute-start.9 = (f32[304,128]{1,0:T(8,128)S(1)}, f32[304,128]{1,0:T(8,128)S(1)}, u32[]{:S(2)}, u32[]{:S(2)}) collective-permute-start(f32[304,128]{1,0:T(8,128)S(1)} %relay.3), channel_id=1, source_target_pairs={{0,24},{4,0},{8,12},{12,8},{16,20},{20,16},{24,28},{28,4},{1,25},{... | collective-permute-start | bytes 466952 | tf_op jit(solution)/shard_map/ppermute | solution.py:351
  22.2 0.0 collective-permute-done.5.refs_3_.came_ref
  22.2 0.0 collective-permute-done.7.refs_5_.refs_1_
  22.3 1.1 %collective-permute-start.8 = (f32[304,128]{1,0:T(8,128)S(1)}, f32[304,128]{1,0:T(8,128)S(1)}, u32[]{:S(2)}, u32[]{:S(2)}) collective-permute-start(f32[304,128]{1,0:T(8,128)S(1)} %relay.2), channel_id=1, source_target_pairs={{0,20},{4,0},{8,12},{12,8},{16,4},{20,16},{24,28},{28,24},{1,21},{... | collective-permute-start | bytes 466952 | tf_op jit(solution)/shard_map/ppermute | solution.py:351
  23.4 0.0 collective-permute-done.2.refs_2_
  23.4 0.0 collective-permute-start.3
  23.4 0.0 copy-start.2
  23.4 0.1 assemble_rows.1
  23.5 0.0 collective-permute-done.1.refs_1_
  23.6 1.4 %collective-permute-done.3.refs_3_ = f32[512,128]{1,0:T(8,128)S(1)} collective-permute-done((f32[512,128]{1,0:T(8,128)S(1)}, f32[512,128]{1,0:T(8,128)S(1)}, u32[]{:S(2)}, u32[]{:S(2)}) %collective-permute-start.3) | collective-permute-done | bytes 262176 | tf_op jit(solution)/shard_map/ppermute | solution.py:287
  24.9 0.0 copy-done.2
  24.9 1.7 %left_factor.1 = (bf16[512,480]{1,0:T(8,128)(2,1)S(1)}, bf16[512,480]{1,0:T(8,128)(2,1)S(1)}, bf16[512,160]{1,0:T(8,128)(2,1)S(1)}, bf16[512,160]{1,0:T(8,128)(2,1)S(1)}, f32[512,512]{1,0:T(8,128)S(1)}) custom-call(s32[1]{0:T(128)} %bitcast.me_ref, s32[1]{0:T(128)} %bitcast.1.col_ref, s32[1,512]{1,0:T(1,128)S(1)} %bitcast.4, f32[512,512]{1,0:T(8,128)S(1)} %copy-done, ...), custom_call_target="tpu_custom_call" | custom-call | flops 1000000000 | tf_op jit(solution)/shard_map/left_factor/pallas_call | solution.py:316
  26.7 1.0 %early_rows.1.base_ref = f32[512,512]{1,0:T(8,128)S(1)} custom-call(bf16[512,480]{1,0:T(8,128)(2,1)S(1)} %get-tuple-element.23.high_ref, bf16[512,480]{1,0:T(8,128)(2,1)S(1)} %get-tuple-element.24.low_ref, f32[512,512]{1,0:T(8,128)S(1)} %get-tuple-element.25.kept_ref, bf16[480,512]{1,0:T(8,128)(2,1)S(1)} %get-tuple-element.31.high_rows, ...), custom_call_target="tpu_custom_call" | custom-call | tf_op jit(solution)/shard_map/early_rows/pallas_call | solution.py:363
  27.7 0.0 collective-permute-done.9.refs_1_
  27.7 1.5 %collective-permute-done.8.refs_0_ = f32[304,128]{1,0:T(8,128)S(1)} collective-permute-done((f32[304,128]{1,0:T(8,128)S(1)}, f32[304,128]{1,0:T(8,128)S(1)}, u32[]{:S(2)}, u32[]{:S(2)}) %collective-permute-start.8) | collective-permute-done | bytes 155680 | tf_op jit(solution)/shard_map/ppermute | solution.py:351
  29.2 1.3 %late_rows.1 = f32[512,512]{1,0:T(8,128)} custom-call(bf16[512,160]{1,0:T(8,128)(2,1)S(1)} %get-tuple-element.21.high_ref, bf16[512,160]{1,0:T(8,128)(2,1)S(1)} %get-tuple-element.22.low_ref, f32[512,512]{1,0:T(8,128)S(1)} %early_rows.1.base_ref, f32[304,128]{1,0:T(8,128)S(1)} %collective-permute-done.8.refs_0_, f32[304,128]{1,0:T(8,128)S(1)} %collective-permute-done.9.refs_1_), custom_call_target="tpu_custom_call" | custom-call | tf_op jit(solution)/shard_map/late_rows/pallas_call | solution.py:371
  (3 shorter events, 0.1 us)
Async XLA Ops:
  0.0 0.7 %copy-start.3 = (s32[512]{0:T(512)S(1)}, s32[512]{0:T(512)}, u32[]{:S(2)}) copy-start(s32[512]{0:T(512)} %param.7) | copy-start | bytes 6148
  0.7 1.2 %copy-start = (f32[512,512]{1,0:T(8,128)S(1)}, f32[512,512]{1,0:T(8,128)}, u32[]{:S(2)}) copy-start(f32[512,512]{1,0:T(8,128)} %slab_ref.3) | copy-start | bytes 3145732
  1.9 10.5 %copy-start.1 = (f32[512,128]{1,0:T(8,128)S(1)}, f32[512,128]{1,0:T(8,128)}, u32[]{:S(2)}) copy-start(f32[512,128]{1,0:T(8,128)} %panel_ref.1) | copy-start | bytes 786436
  2.9 9.5 %collective-permute-start = (f32[304,128]{1,0:T(8,128)S(1)}, f32[304,128]{1,0:T(8,128)S(1)}, u32[]{:S(2)}, u32[]{:S(2)}) collective-permute-start(f32[304,128]{1,0:T(8,128)S(1)} %get-tuple-element.20), channel_id=1, source_target_pairs={{0,8},{4,12},{8,0},{12,4},{16,24},{20,28},{24,16},{28,20},{1,9},{5... | collective-permute-start | bytes 466952 | tf_op jit(solution)/shard_map/ppermute | solution.py:287
  5.6 11.8 %collective-permute-start.6 = (f32[304,128]{1,0:T(8,128)S(1)}, f32[304,128]{1,0:T(8,128)S(1)}, u32[]{:S(2)}, u32[]{:S(2)}) collective-permute-start(f32[304,128]{1,0:T(8,128)S(1)} %get-tuple-element.29), channel_id=1, source_target_pairs={{0,28},{4,24},{8,16},{12,20},{16,8},{20,12},{24,4},{28,0},{1,29},{... | collective-permute-start | bytes 466952 | tf_op jit(solution)/shard_map/ppermute | solution.py:295
  9.0 11.9 %collective-permute-start.4 = (f32[304,128]{1,0:T(8,128)S(1)}, f32[304,128]{1,0:T(8,128)S(1)}, u32[]{:S(2)}, u32[]{:S(2)}) collective-permute-start(f32[304,128]{1,0:T(8,128)S(1)} %get-tuple-element.27), channel_id=1, source_target_pairs={{0,4},{4,0},{8,12},{12,8},{16,20},{20,16},{24,28},{28,24},{1,5},{5... | collective-permute-start | bytes 466952 | tf_op jit(solution)/shard_map/ppermute | solution.py:287
  9.5 12.7 %collective-permute-start.5 = (f32[304,128]{1,0:T(8,128)S(1)}, f32[304,128]{1,0:T(8,128)S(1)}, u32[]{:S(2)}, u32[]{:S(2)}) collective-permute-start(f32[304,128]{1,0:T(8,128)S(1)} %get-tuple-element.28), channel_id=1, source_target_pairs={{0,16},{4,20},{8,24},{12,28},{16,0},{20,4},{24,8},{28,12},{1,17},{... | collective-permute-start | bytes 466952 | tf_op jit(solution)/shard_map/ppermute | solution.py:287
  9.7 12.5 %collective-permute-start.7 = (f32[304,128]{1,0:T(8,128)S(1)}, f32[304,128]{1,0:T(8,128)S(1)}, u32[]{:S(2)}, u32[]{:S(2)}) collective-permute-start(f32[304,128]{1,0:T(8,128)S(1)} %get-tuple-element.30), channel_id=1, source_target_pairs={{0,12},{4,8},{8,4},{12,0},{16,28},{20,24},{24,20},{28,16},{1,13},{... | collective-permute-start | bytes 466952 | tf_op jit(solution)/shard_map/ppermute | solution.py:287
  12.4 11.0 %collective-permute-start.2 = (f32[512,128]{1,0:T(8,128)S(1)}, f32[512,128]{1,0:T(8,128)S(1)}, u32[]{:S(2)}, u32[]{:S(2)}) collective-permute-start(f32[512,128]{1,0:T(8,128)S(1)} %panel_after.1.refs_0_), channel_id=1, source_target_pairs={{0,2},{1,3},{2,0},{3,1},{4,6},{5,7},{6,4},{7,5},{8,10},{9,11},{10,... | collective-permute-start | bytes 786440 | tf_op jit(solution)/shard_map/ppermute | solution.py:287
  17.4 6.2 %collective-permute-start.1 = (f32[512,128]{1,0:T(8,128)S(1)}, f32[512,128]{1,0:T(8,128)S(1)}, u32[]{:S(2)}, u32[]{:S(2)}) collective-permute-start(f32[512,128]{1,0:T(8,128)S(1)} %panel_after.1.refs_0_), channel_id=1, source_target_pairs={{0,1},{1,0},{2,3},{3,2},{4,5},{5,4},{6,7},{7,6},{8,9},{9,8},{10,11... | collective-permute-start | bytes 786440 | tf_op jit(solution)/shard_map/ppermute | solution.py:287
  20.9 6.8 %collective-permute-start.9 = (f32[304,128]{1,0:T(8,128)S(1)}, f32[304,128]{1,0:T(8,128)S(1)}, u32[]{:S(2)}, u32[]{:S(2)}) collective-permute-start(f32[304,128]{1,0:T(8,128)S(1)} %relay.3), channel_id=1, source_target_pairs={{0,24},{4,0},{8,12},{12,8},{16,20},{20,16},{24,28},{28,4},{1,25},{... | collective-permute-start | bytes 466952 | tf_op jit(solution)/shard_map/ppermute | solution.py:351
  22.3 6.9 %collective-permute-start.8 = (f32[304,128]{1,0:T(8,128)S(1)}, f32[304,128]{1,0:T(8,128)S(1)}, u32[]{:S(2)}, u32[]{:S(2)}) collective-permute-start(f32[304,128]{1,0:T(8,128)S(1)} %relay.2), channel_id=1, source_target_pairs={{0,20},{4,0},{8,12},{12,8},{16,4},{20,16},{24,28},{28,24},{1,21},{... | collective-permute-start | bytes 466952 | tf_op jit(solution)/shard_map/ppermute | solution.py:351
  23.4 1.5 %collective-permute-start.3 = (f32[512,128]{1,0:T(8,128)S(1)}, f32[512,128]{1,0:T(8,128)S(1)}, u32[]{:S(2)}, u32[]{:S(2)}) collective-permute-start(f32[512,128]{1,0:T(8,128)S(1)} %collective-permute-done.2.refs_2_), channel_id=1, source_target_pairs={{0,1},{1,0},{2,3},{3,2},{4,5},{5,4},{6,7},{7,6},{8,9},{9,8},{10,11... | collective-permute-start | bytes 786440 | tf_op jit(solution)/shard_map/ppermute | solution.py:287
  23.4 1.5 %copy-start.2 = (f32[512,512]{1,0:T(8,128)S(1)}, f32[512,512]{1,0:T(8,128)}, u32[]{:S(2)}) copy-start(f32[512,512]{1,0:T(8,128)} %tri_ref.1) | copy-start | bytes 3145732
where the time goes:
time: 30.7 us; the launch traced here: 30.5 us
  starting transfers between devices  13.6 us (44%)
  waiting for transfers between devices  9.78 us (32%)
  Pallas kernels  5.49 us (18%)
  local copies, waits for them, and re-layouts  1.6 us (5%)
    ppermute x7, starting transfers between devices, swap(): return lax.ppermute(x, axis, [(i, i ^ step) for i in range(size)])  7.68 us
    ppermute x7, waiting for transfers between devices, swap(): return lax.ppermute(x, axis, [(i, i ^ step) for i in range(size)])  4.85 us
    ppermute x1, starting transfers between devices, per_device(): rows[step] = lax.ppermute(outgoing[step ^ 1], 'prow', pairs)  3.4 us
    ppermute x1, waiting for transfers between devices, per_device(): rows[step] = lax.ppermute(outgoing[step ^ 1], 'prow', pairs)  3.39 us
    ppermute x2, starting transfers between devices, per_device(): rows[other] = lax.ppermute(passed, 'prow', pairs)  2.48 us
    pallas_call x1, Pallas kernels, per_device(): pl.pallas_call(functools.partial(_factor_kernel, devices, block, order, e...  1.74 us
    unnamed x8, local copies, waits for them, and re-layouts  1.6 us
    ppermute x2, waiting for transfers between devices, per_device(): rows[other] = lax.ppermute(passed, 'prow', pairs)  1.53 us
  transfers between devices with their start and end apart: 10, of which 4 were waited for; matrix products, arithmetic and copies ran while one was open for 0% of the time, Pallas kernels for 10%

commit v1 on v0

--- a/solution.py
+++ b/solution.py
@@ -231,9 +231,12 @@
     out_ref[...] = kept_ref[...] + _product(high_ref[...], low_ref[...], high_rows[...], low_rows[...])
 
 
-def _late_kernel(block, packing, blocks, high_ref, low_ref, base_ref, *refs):
-    out_hbm, high_rows, low_rows, result, sems = refs[blocks:]
-    _split_rows(block, packing, refs[:blocks], high_rows, low_rows)
+def _late_kernel(block, packing, late, high_ref, low_ref, base_ref, last_ref, rest_high, rest_low, *refs):
+    out_hbm, high_rows, low_rows, result, sems = refs
+    rest = pl.ds(block, (late - 1) * block)
+    high_rows[rest, :] = rest_high[...]
+    low_rows[rest, :] = rest_low[...]
+    _split_rows(block, packing, [last_ref], high_rows, low_rows)
     high, low = high_rows[...], low_rows[...]
     part = result.shape[0] // STORE_PARTS
     stores = []
@@ -368,16 +371,25 @@
         compiler_params=params,
         name="early_rows",
     )(high_early, low_early, kept, high_rows, low_rows)
+    rest_high, rest_low = pl.pallas_call(
+        functools.partial(_assemble_kernel, block, packing, late - 1),
+        out_shape=[jax.ShapeDtypeStruct(((late - 1) * block, cols_dev), BF16)] * 2,
+        in_specs=[vmem] * (late - 1),
+        out_specs=[vmem] * 2,
+        compiler_params=params,
+        cost_estimate=_cost(AFTER_US),
+        name="assemble_late",
+    )(*[rows[s] for s in order[early + 1 :]])
     return pl.pallas_call(
         functools.partial(_late_kernel, block, packing, late),
         out_shape=result_type,
-        in_specs=[vmem] * (3 + late),
+        in_specs=[vmem] * 6,
         out_specs=hbm,
         scratch_shapes=[pltpu.VMEM((late * block, cols_dev), BF16)] * 2
         + [pltpu.VMEM((rows_dev, cols_dev), F32), pltpu.SemaphoreType.DMA((STORE_PARTS,))],
         compiler_params=params,
         name="late_rows",
-    )(high_late, low_late, partial, *[rows[s] for s in order[early:]])
+    )(high_late, low_late, partial, rows[order[early]], rest_high, rest_low)
 
 
 def solution(mesh):

time: 30.7 us -> 31.8 us (1.036)
  waiting for transfers between devices: 9.78 us -> 10.9 us
    ppermute x2, waiting for transfers between devices: 1.53 us -> 3.99 us  [per_device(): rows[other] = lax.ppermute(passed, 'prow', pairs)]
    ppermute x7, waiting for transfers between devices: 4.85 us -> 3.48 us  [swap(): return lax.ppermute(x, axis, [(i, i ^ step) for i in range(size)])]
  transfers between devices with their start and end apart: 10 -> 10, of which waited for: 4 -> 3; matrix products, arithmetic and copies ran while one was open for 0% -> 0% of each run, Pallas kernels for 10% -> 9%
where the time goes in v1:
time: 31.8 us; the launch traced here: 31.7 us
  starting transfers between devices  13.6 us (43%)
  waiting for transfers between devices  10.9 us (34%)
  Pallas kernels  5.53 us (17%)
  local copies, waits for them, and re-layouts  1.6 us (5%)
    ppermute x7, starting transfers between devices, swap(): return lax.ppermute(x, axis, [(i, i ^ step) for i in range(size)])  7.68 us
    ppermute x2, waiting for transfers between devices, per_device(): rows[other] = lax.ppermute(passed, 'prow', pairs)  3.99 us
    ppermute x7, waiting for transfers between devices, swap(): return lax.ppermute(x, axis, [(i, i ^ step) for i in range(size)])  3.48 us
    ppermute x1, starting transfers between devices, per_device(): rows[step] = lax.ppermute(outgoing[step ^ 1], 'prow', pairs)  3.4 us
    ppermute x1, waiting for transfers between devices, per_device(): rows[step] = lax.ppermute(outgoing[step ^ 1], 'prow', pairs)  3.39 us
    ppermute x2, starting transfers between devices, per_device(): rows[other] = lax.ppermute(passed, 'prow', pairs)  2.48 us
    pallas_call x1, Pallas kernels, per_device(): pl.pallas_call(functools.partial(_factor_kernel, devices, block, order, e...  1.75 us
    unnamed x8, local copies, waits for them, and re-layouts  1.6 us
  transfers between devices with their start and end apart: 10, of which 3 were waited for; matrix products, arithmetic and copies ran while one was open for 0% of the time, Pallas kernels for 9%

profile of v1, /device:TPU:0, one launch (start us, length us, event | category | flops | bytes accessed | tf_op | source)
XLA Modules:
  0.0 31.7 jit_solution(1076998243031119414)
XLA Ops:
  0.0 0.0 copy-start.3
  0.0 0.7 %copy-done.3 = s32[512]{0:T(512)S(1)} copy-done((s32[512]{0:T(512)S(1)}, s32[512]{0:T(512)}, u32[]{:S(2)}) %copy-start.3) | copy-done | bytes 2072
  0.7 0.0 copy-start
  0.7 0.3 pick_rows.1.pick_ref
  1.0 0.9 %copy-done = f32[512,512]{1,0:T(8,128)S(1)} copy-done((f32[512,512]{1,0:T(8,128)S(1)}, f32[512,512]{1,0:T(8,128)}, u32[]{:S(2)}) %copy-start) | copy-done | bytes 1048600
  1.9 0.0 copy-start.1
  1.9 1.0 %outgoing_rows.1 = (f32[80,512]{1,0:T(8,128)S(1)}, f32[304,128]{1,0:T(8,128)S(1)}, f32[304,128]{1,0:T(8,128)S(1)}, f32[304,128]{1,0:T(8,128)S(1)}, f32[304,128]{...) custom-call(s32[1]{0:T(128)} %bitcast.me_ref, ...), custom_call_target="tpu_custom_call" | custom-call | tf_op jit(solution)/shard_map/outgoing_rows/pallas_call | solution.py:280
  2.9 2.7 %collective-permute-start = (f32[304,128]{1,0:T(8,128)S(1)}, f32[304,128]{1,0:T(8,128)S(1)}, u32[]{:S(2)}, u32[]{:S(2)}) collective-permute-start(f32[304,128]{1,0:T(8,128)S(1)} %get-tuple-element.22), channel_id=1, source_target_pairs={{0,8},{4,12},{8,0},{12,4},{16,24},{20,28},{24,16},{28,20},{1,9},{5... | collective-permute-start | bytes 466952 | tf_op jit(solution)/shard_map/ppermute | solution.py:290
  5.6 3.4 %collective-permute-start.6 = (f32[304,128]{1,0:T(8,128)S(1)}, f32[304,128]{1,0:T(8,128)S(1)}, u32[]{:S(2)}, u32[]{:S(2)}) collective-permute-start(f32[304,128]{1,0:T(8,128)S(1)} %get-tuple-element.31), channel_id=1, source_target_pairs={{0,28},{4,24},{8,16},{12,20},{16,8},{20,12},{24,4},{28,0},{1,29},{... | collective-permute-start | bytes 466952 | tf_op jit(solution)/shard_map/ppermute | solution.py:298
  9.0 0.5 %collective-permute-start.4 = (f32[304,128]{1,0:T(8,128)S(1)}, f32[304,128]{1,0:T(8,128)S(1)}, u32[]{:S(2)}, u32[]{:S(2)}) collective-permute-start(f32[304,128]{1,0:T(8,128)S(1)} %get-tuple-element.29), channel_id=1, source_target_pairs={{0,4},{4,0},{8,12},{12,8},{16,20},{20,16},{24,28},{28,24},{1,5},{5... | collective-permute-start | bytes 466952 | tf_op jit(solution)/shard_map/ppermute | solution.py:290
  9.5 0.1 collective-permute-start.5
  9.7 2.7 %collective-permute-start.7 = (f32[304,128]{1,0:T(8,128)S(1)}, f32[304,128]{1,0:T(8,128)S(1)}, u32[]{:S(2)}, u32[]{:S(2)}) collective-permute-start(f32[304,128]{1,0:T(8,128)S(1)} %get-tuple-element.32), channel_id=1, source_target_pairs={{0,12},{4,8},{8,4},{12,0},{16,28},{20,24},{24,20},{28,16},{1,13},{... | collective-permute-start | bytes 466952 | tf_op jit(solution)/shard_map/ppermute | solution.py:290
  12.4 0.0 collective-permute-done._.refs_2_
  12.4 0.0 copy-done.1
  12.4 1.6 %collective-permute-start.2 = (f32[512,128]{1,0:T(8,128)S(1)}, f32[512,128]{1,0:T(8,128)S(1)}, u32[]{:S(2)}, u32[]{:S(2)}) collective-permute-start(f32[512,128]{1,0:T(8,128)S(1)} %panel_after.1.refs_0_), channel_id=1, source_target_pairs={{0,2},{1,3},{2,0},{3,1},{4,6},{5,7},{6,4},{7,5},{8,10},{9,11},{10,... | collective-permute-start | bytes 786440 | tf_op jit(solution)/shard_map/ppermute | solution.py:290
  14.0 3.4 %collective-permute-done.6.refs_4_.came_ref = f32[304,128]{1,0:T(8,128)S(1)} collective-permute-done((f32[304,128]{1,0:T(8,128)S(1)}, f32[304,128]{1,0:T(8,128)S(1)}, u32[]{:S(2)}, u32[]{:S(2)}) %collective-permute-start.6) | collective-permute-done | bytes 155680 | tf_op jit(solution)/shard_map/ppermute | solution.py:298
  17.4 0.0 collective-permute-start.1
  17.4 3.5 %collective-permute-done.4.refs_1_.refs_0_ = f32[304,128]{1,0:T(8,128)S(1)} collective-permute-done((f32[304,128]{1,0:T(8,128)S(1)}, f32[304,128]{1,0:T(8,128)S(1)}, u32[]{:S(2)}, u32[]{:S(2)}) %collective-permute-start.4) | collective-permute-done | bytes 155680 | tf_op jit(solution)/shard_map/ppermute | solution.py:290
  20.9 1.3 %collective-permute-start.9 = (f32[304,128]{1,0:T(8,128)S(1)}, f32[304,128]{1,0:T(8,128)S(1)}, u32[]{:S(2)}, u32[]{:S(2)}) collective-permute-start(f32[304,128]{1,0:T(8,128)S(1)} %relay.3), channel_id=1, source_target_pairs={{0,24},{4,0},{8,12},{12,8},{16,20},{20,16},{24,28},{28,4},{1,25},{... | collective-permute-start | bytes 466952 | tf_op jit(solution)/shard_map/ppermute | solution.py:354
  22.2 0.0 collective-permute-done.5.refs_3_.came_ref
  22.2 0.0 collective-permute-done.7.refs_5_.refs_1_
  22.3 1.1 %collective-permute-start.8 = (f32[304,128]{1,0:T(8,128)S(1)}, f32[304,128]{1,0:T(8,128)S(1)}, u32[]{:S(2)}, u32[]{:S(2)}) collective-permute-start(f32[304,128]{1,0:T(8,128)S(1)} %relay.2), channel_id=1, source_target_pairs={{0,20},{4,0},{8,12},{12,8},{16,4},{20,16},{24,28},{28,24},{1,21},{... | collective-permute-start | bytes 466952 | tf_op jit(solution)/shard_map/ppermute | solution.py:354
  23.4 0.0 collective-permute-done.2.refs_2_
  23.4 0.0 collective-permute-start.3
  23.4 0.0 copy-start.2
  23.4 0.1 assemble_rows.1
  23.5 4.0 %collective-permute-done.9.refs_0_ = f32[304,128]{1,0:T(8,128)S(1)} collective-permute-done((f32[304,128]{1,0:T(8,128)S(1)}, f32[304,128]{1,0:T(8,128)S(1)}, u32[]{:S(2)}, u32[]{:S(2)}) %collective-permute-start.9) | collective-permute-done | bytes 155680 | tf_op jit(solution)/shard_map/ppermute | solution.py:354
  27.6 0.0 collective-permute-done.1.refs_1_
  27.6 0.0 collective-permute-done.3.refs_3_
  27.6 0.0 copy-done.2
  27.6 1.7 %left_factor.1 = (bf16[512,480]{1,0:T(8,128)(2,1)S(1)}, bf16[512,480]{1,0:T(8,128)(2,1)S(1)}, bf16[512,160]{1,0:T(8,128)(2,1)S(1)}, bf16[512,160]{1,0:T(8,128)(2,1)S(1)}, f32[512,512]{1,0:T(8,128)S(1)}) custom-call(s32[1]{0:T(128)} %bitcast.me_ref, s32[1]{0:T(128)} %bitcast.1.col_ref, s32[1,512]{1,0:T(1,128)S(1)} %bitcast.4, f32[512,512]{1,0:T(8,128)S(1)} %copy-done, ...), custom_call_target="tpu_custom_call" | custom-call | flops 1000000000 | tf_op jit(solution)/shard_map/left_factor/pallas_call | solution.py:319
  29.4 1.0 %early_rows.1.base_ref = f32[512,512]{1,0:T(8,128)S(1)} custom-call(bf16[512,480]{1,0:T(8,128)(2,1)S(1)} %get-tuple-element.25.high_ref, bf16[512,480]{1,0:T(8,128)(2,1)S(1)} %get-tuple-element.26.low_ref, f32[512,512]{1,0:T(8,128)S(1)} %get-tuple-element.27.kept_ref, bf16[480,512]{1,0:T(8,128)(2,1)S(1)} %get-tuple-element.33.high_rows, ...), custom_call_target="tpu_custom_call" | custom-call | tf_op jit(solution)/shard_map/early_rows/pallas_call | solution.py:366
  30.3 0.0 collective-permute-done.8.last_ref
  30.3 1.3 %late_rows.1 = f32[512,512]{1,0:T(8,128)} custom-call(bf16[512,160]{1,0:T(8,128)(2,1)S(1)} %get-tuple-element.23.high_ref, bf16[512,160]{1,0:T(8,128)(2,1)S(1)} %get-tuple-element.24.low_ref, f32[512,512]{1,0:T(8,128)S(1)} %early_rows.1.base_ref, f32[304,128]{1,0:T(8,128)S(1)} %collective-permute-done.8.last_ref, ...), custom_call_target="tpu_custom_call" | custom-call | tf_op jit(solution)/shard_map/late_rows/pallas_call | solution.py:383
  (4 shorter events, 0.1 us)
Async XLA Ops:
  0.0 0.7 %copy-start.3 = (s32[512]{0:T(512)S(1)}, s32[512]{0:T(512)}, u32[]{:S(2)}) copy-start(s32[512]{0:T(512)} %param.7) | copy-start | bytes 6148
  0.7 1.2 %copy-start = (f32[512,512]{1,0:T(8,128)S(1)}, f32[512,512]{1,0:T(8,128)}, u32[]{:S(2)}) copy-start(f32[512,512]{1,0:T(8,128)} %slab_ref.3) | copy-start | bytes 3145732
  1.9 10.5 %copy-start.1 = (f32[512,128]{1,0:T(8,128)S(1)}, f32[512,128]{1,0:T(8,128)}, u32[]{:S(2)}) copy-start(f32[512,128]{1,0:T(8,128)} %panel_ref.1) | copy-start | bytes 786436
  2.9 9.5 %collective-permute-start = (f32[304,128]{1,0:T(8,128)S(1)}, f32[304,128]{1,0:T(8,128)S(1)}, u32[]{:S(2)}, u32[]{:S(2)}) collective-permute-start(f32[304,128]{1,0:T(8,128)S(1)} %get-tuple-element.22), channel_id=1, source_target_pairs={{0,8},{4,12},{8,0},{12,4},{16,24},{20,28},{24,16},{28,20},{1,9},{5... | collective-permute-start | bytes 466952 | tf_op jit(solution)/shard_map/ppermute | solution.py:290
  5.6 11.8 %collective-permute-start.6 = (f32[304,128]{1,0:T(8,128)S(1)}, f32[304,128]{1,0:T(8,128)S(1)}, u32[]{:S(2)}, u32[]{:S(2)}) collective-permute-start(f32[304,128]{1,0:T(8,128)S(1)} %get-tuple-element.31), channel_id=1, source_target_pairs={{0,28},{4,24},{8,16},{12,20},{16,8},{20,12},{24,4},{28,0},{1,29},{... | collective-permute-start | bytes 466952 | tf_op jit(solution)/shard_map/ppermute | solution.py:298
  9.0 11.9 %collective-permute-start.4 = (f32[304,128]{1,0:T(8,128)S(1)}, f32[304,128]{1,0:T(8,128)S(1)}, u32[]{:S(2)}, u32[]{:S(2)}) collective-permute-start(f32[304,128]{1,0:T(8,128)S(1)} %get-tuple-element.29), channel_id=1, source_target_pairs={{0,4},{4,0},{8,12},{12,8},{16,20},{20,16},{24,28},{28,24},{1,5},{5... | collective-permute-start | bytes 466952 | tf_op jit(solution)/shard_map/ppermute | solution.py:290
  9.5 12.7 %collective-permute-start.5 = (f32[304,128]{1,0:T(8,128)S(1)}, f32[304,128]{1,0:T(8,128)S(1)}, u32[]{:S(2)}, u32[]{:S(2)}) collective-permute-start(f32[304,128]{1,0:T(8,128)S(1)} %get-tuple-element.30), channel_id=1, source_target_pairs={{0,16},{4,20},{8,24},{12,28},{16,0},{20,4},{24,8},{28,12},{1,17},{... | collective-permute-start | bytes 466952 | tf_op jit(solution)/shard_map/ppermute | solution.py:290
  9.7 12.5 %collective-permute-start.7 = (f32[304,128]{1,0:T(8,128)S(1)}, f32[304,128]{1,0:T(8,128)S(1)}, u32[]{:S(2)}, u32[]{:S(2)}) collective-permute-start(f32[304,128]{1,0:T(8,128)S(1)} %get-tuple-element.32), channel_id=1, source_target_pairs={{0,12},{4,8},{8,4},{12,0},{16,28},{20,24},{24,20},{28,16},{1,13},{... | collective-permute-start | bytes 466952 | tf_op jit(solution)/shard_map/ppermute | solution.py:290
  12.4 11.0 %collective-permute-start.2 = (f32[512,128]{1,0:T(8,128)S(1)}, f32[512,128]{1,0:T(8,128)S(1)}, u32[]{:S(2)}, u32[]{:S(2)}) collective-permute-start(f32[512,128]{1,0:T(8,128)S(1)} %panel_after.1.refs_0_), channel_id=1, source_target_pairs={{0,2},{1,3},{2,0},{3,1},{4,6},{5,7},{6,4},{7,5},{8,10},{9,11},{10,... | collective-permute-start | bytes 786440 | tf_op jit(solution)/shard_map/ppermute | solution.py:290
  17.4 10.2 %collective-permute-start.1 = (f32[512,128]{1,0:T(8,128)S(1)}, f32[512,128]{1,0:T(8,128)S(1)}, u32[]{:S(2)}, u32[]{:S(2)}) collective-permute-start(f32[512,128]{1,0:T(8,128)S(1)} %panel_after.1.refs_0_), channel_id=1, source_target_pairs={{0,1},{1,0},{2,3},{3,2},{4,5},{5,4},{6,7},{7,6},{8,9},{9,8},{10,11... | collective-permute-start | bytes 786440 | tf_op jit(solution)/shard_map/ppermute | solution.py:290
  20.9 6.7 %collective-permute-start.9 = (f32[304,128]{1,0:T(8,128)S(1)}, f32[304,128]{1,0:T(8,128)S(1)}, u32[]{:S(2)}, u32[]{:S(2)}) collective-permute-start(f32[304,128]{1,0:T(8,128)S(1)} %relay.3), channel_id=1, source_target_pairs={{0,24},{4,0},{8,12},{12,8},{16,20},{20,16},{24,28},{28,4},{1,25},{... | collective-permute-start | bytes 466952 | tf_op jit(solution)/shard_map/ppermute | solution.py:354
  22.3 8.1 %collective-permute-start.8 = (f32[304,128]{1,0:T(8,128)S(1)}, f32[304,128]{1,0:T(8,128)S(1)}, u32[]{:S(2)}, u32[]{:S(2)}) collective-permute-start(f32[304,128]{1,0:T(8,128)S(1)} %relay.2), channel_id=1, source_target_pairs={{0,20},{4,0},{8,12},{12,8},{16,4},{20,16},{24,28},{28,24},{1,21},{... | collective-permute-start | bytes 466952 | tf_op jit(solution)/shard_map/ppermute | solution.py:354
  23.4 4.2 %collective-permute-start.3 = (f32[512,128]{1,0:T(8,128)S(1)}, f32[512,128]{1,0:T(8,128)S(1)}, u32[]{:S(2)}, u32[]{:S(2)}) collective-permute-start(f32[512,128]{1,0:T(8,128)S(1)} %collective-permute-done.2.refs_2_), channel_id=1, source_target_pairs={{0,1},{1,0},{2,3},{3,2},{4,5},{5,4},{6,7},{7,6},{8,9},{9,8},{10,11... | collective-permute-start | bytes 786440 | tf_op jit(solution)/shard_map/ppermute | solution.py:290
  23.4 4.2 %copy-start.2 = (f32[512,512]{1,0:T(8,128)S(1)}, f32[512,512]{1,0:T(8,128)}, u32[]{:S(2)}) copy-start(f32[512,512]{1,0:T(8,128)} %tri_ref.1) | copy-start | bytes 3145732
